TPU v7x, 32 devices: a whole 2x2x4 slice. The times are simulated.
32 devices in a mesh: ctx: 4 (over y, x), head: 8 (over z, core).
Axes of the slice: x: 2, y: 2, z: 4, core: 2. Of those that a mesh axis runs over, the one named last changes fastest.
Arguments:
- hidden_in: bfloat16 [4096, 5376], P(('ctx', 'head')), may hold values from -6 to 6
- pre_gain: float32 [5376], replicated, may hold values from 0.1 to 1.9
- w_query: bfloat16 [5376, 4096], P('ctx', 'head'), may hold values from -0.054554473 to 0.054554473, as said below
- w_key: bfloat16 [5376, 2048], P('ctx', 'head'), may hold values from -0.054554473 to 0.054554473, as said below
- value_weight: bfloat16 [5376, 2048], P('ctx', 'head'), may hold values from -0.078125 to 0.078125
- query_gain: float32 [128], replicated, may hold values from 0.6 to 7, as said below
- key_norm_gain: float32 [128], replicated, may hold values from 0.6 to 7, as said below
- w_output: bfloat16 [4096, 5376], P(('head', 'ctx')), may hold values from -0.09375 to 0.09375
- post_gain: float32 [5376], replicated, may hold values from 0.1 to 1.9
Outputs:
- layer_out: bfloat16 [4096, 5376], P(('ctx', 'head'))
Inputs may be any that keep to these rules, and one draw needn't show every extreme that they name: `w_query`: entries are normal draws clipped to 4 standard deviations, scaled by 5376 ** -0.5. `w_key`: entries are normal draws clipped to 4 standard deviations, scaled by 5376 ** -0.5. `query_gain`: positive gains. `key_norm_gain`: positive gains.
All inputs are finite; a program needn't handle non-finite values.
Results may differ from a plain program's by a relative error of at most 0.015.
The roundings to bfloat16 on the way count: a program that leaves them out, or rounds other values in their place, can miss the bound.
Values may be sent and summed in bfloat16 or wider, within the bound.
A program may use at most 128 MiB of HBM per device.

v0:
```python
import jax
import jax.numpy as jnp
from jax import lax
from jax.sharding import PartitionSpec as P

HEAD_SIZE = 128
WINDOW_SPAN = 1024


norm_eps = 1e-06
query_scale = 168.0 ** (-0.5)
rope_base = 10000.0
mask_value = -1e30


def passed_along(shard, axis, by):
    count = lax.axis_size(axis)
    pairs = [(i, i + by) for i in range(count) if 0 <= i + by < count]
    return lax.ppermute(shard, axis, pairs)


def root_mean_scale(values, scaling):
    mean_sq = jnp.mean(values * values, axis=-1, keepdims=True)
    return values * lax.rsqrt(mean_sq + norm_eps) * scaling


def apply_rotary(values, token_places):
    full_width = values.shape[-1]
    half_width = full_width // 2
    frequency = rope_base ** (-jnp.arange(half_width, dtype=jnp.float32) * 2.0 / full_width)
    angles = token_places.astype(jnp.float32)[:, None] * frequency[None, :]
    cosine = jnp.cos(angles)[:, None, :]
    sine_part = jnp.sin(angles)[:, None, :]
    lower_half = values[..., :half_width]
    upper_half = values[..., half_width:]
    return jnp.concatenate(
        [
            lower_half * cosine - upper_half * sine_part,
            upper_half * cosine + lower_half * sine_part,
        ],
        axis=-1,
    )


def body(
    hidden_in,
    pre_gain,
    w_query,
    w_key,
    value_weight,
    query_gain,
    key_norm_gain,
    w_output,
    post_gain,
):
    own_rows = hidden_in.astype(jnp.float32)
    raw_rows = lax.all_gather(hidden_in, "head", axis=0, tiled=True)
    normed = root_mean_scale(raw_rows.astype(jnp.float32), pre_gain).astype(jnp.bfloat16)
    tok_count = normed.shape[0]

    def add_rows(weight_piece):
        return jnp.dot(normed, weight_piece, preferred_element_type=jnp.float32)

    query_raw = add_rows(lax.all_gather(w_query, "ctx", axis=0, tiled=True))
    key_unnormed = add_rows(lax.all_gather(w_key, "ctx", axis=0, tiled=True))
    value_unnormed = add_rows(lax.all_gather(value_weight, "ctx", axis=0, tiled=True))
    local_heads = w_query.shape[1] // HEAD_SIZE
    local_groups = w_key.shape[1] // HEAD_SIZE
    heads_per_group = local_heads // local_groups
    ctx_index = lax.axis_index("ctx")
    token_places = ctx_index * tok_count + jnp.arange(tok_count, dtype=jnp.int32)
    query_matrix = (
        apply_rotary(
            root_mean_scale(query_raw.reshape(tok_count, local_heads, HEAD_SIZE), query_gain),
            token_places,
        )
        * query_scale
    ).astype(jnp.bfloat16)
    projected_keys = apply_rotary(
        root_mean_scale(key_unnormed.reshape(tok_count, local_groups, HEAD_SIZE), key_norm_gain),
        token_places,
    ).astype(jnp.bfloat16)
    projected_values = value_unnormed.astype(jnp.bfloat16)
    key_value = jnp.stack(
        [projected_keys.reshape(tok_count, local_groups * HEAD_SIZE), projected_values]
    )
    pieces = [passed_along(key_value, "ctx", 1)]
    extended = jnp.concatenate(pieces + [key_value], axis=1)
    band_keys = extended[0].reshape(-1, local_groups, HEAD_SIZE)
    band_values = extended[1].reshape(-1, local_groups, HEAD_SIZE)
    block_rows = min(512, tok_count)
    grouped_queries = query_matrix.reshape(tok_count, local_groups, heads_per_group, HEAD_SIZE)
    outputs = []
    for block_index in range(tok_count // block_rows):
        first_row = block_index * block_rows
        query_block = grouped_queries[first_row : first_row + block_rows]
        key_block = band_keys[first_row : first_row + block_rows + WINDOW_SPAN]
        value_block = band_values[first_row : first_row + block_rows + WINDOW_SPAN]
        scores = jnp.einsum(
            "qjgd,kjd->jgqk", query_block, key_block, preferred_element_type=jnp.float32
        )
        query_spots = token_places[first_row : first_row + block_rows]
        key_spots = (
            ctx_index * tok_count
            - WINDOW_SPAN
            + first_row
            + jnp.arange(block_rows + WINDOW_SPAN, dtype=jnp.int32)
        )
        allowed = (
            (key_spots[None, :] <= query_spots[:, None])
            & (key_spots[None, :] > query_spots[:, None] - WINDOW_SPAN)
            & (key_spots[None, :] >= 0)
        )
        scores = jnp.where(allowed, scores, mask_value)
        row_max = jnp.max(scores, axis=-1, keepdims=True)
        weights = jnp.exp(scores - row_max)
        row_sum = jnp.sum(weights, axis=-1, keepdims=True)
        probabilities = (weights / row_sum).astype(jnp.bfloat16)
        mixed = jnp.einsum(
            "jgqk,kjd->qjgd", probabilities, value_block, preferred_element_type=jnp.float32
        )
        outputs.append(mixed.astype(jnp.bfloat16).reshape(block_rows, local_heads * HEAD_SIZE))
    attended = jnp.concatenate(outputs, axis=0)
    out_weight = lax.all_gather(w_output, "ctx", axis=0, tiled=True)
    partial_value = jnp.dot(attended, out_weight, preferred_element_type=jnp.float32).astype(
        jnp.bfloat16
    )
    summed = lax.psum_scatter(
        lax.optimization_barrier(partial_value).astype(jnp.float32).astype(jnp.bfloat16),
        "head",
        scatter_dimension=0,
        tiled=True,
    ).astype(jnp.float32)
    result = own_rows + root_mean_scale(summed, post_gain)
    return result.astype(jnp.bfloat16)


def solution(mesh):
    return jax.shard_map(
        body,
        mesh=mesh,
        in_specs=(
            P(("ctx", "head"), None),
            P(),
            P("ctx", "head"),
            P("ctx", "head"),
            P("ctx", "head"),
            P(),
            P(),
            P(("head", "ctx"), None),
            P(),
        ),
        out_specs=P(("ctx", "head"), None),
        check_vma=False,
    )
```

profile of v0, /device:TPU:0, one launch (start us, length us, event | category | flops | bytes accessed | tf_op | source)
XLA Modules:
  0.0 481.3 jit_solution(9102571523680790515)
XLA Ops:
  6.5 0.7 all-gather.6.cloned.1.call-update
  7.3 0.7 all-gather.8.cloned.1.call-update
  8.1 0.7 all-gather.10.cloned.1.call-update
  8.8 0.5 all-gather.12.cloned.1.call-update
  9.4 0.5 all-gather.14.cloned.1.call-update
  10.1 1.0 multiply_cosine_fusion
  11.0 1.9 and_and_fusion.1
  12.9 1.8 and_and_fusion
  14.8 100.7 %all-gather.6.cloned.1.call-done = bf16[1024,5376]{1,0:T(8,128)(2,1)} async-done(((bf16[128,5376]{1,0:T(8,128)(2,1)}), bf16[1024,5376]{1,0:T(8,128)(2,1)}) %all-gather.6.cloned.1.call-update) | async-done | bytes 11010064 | tf_op jit(solution)/shard_map/all_gather | solution.py:57
  115.5 6.3 %fusion.2 = f32[1024]{0:T(1024)S(1)} fusion(bf16[1024,5376]{1,0:T(8,128)(2,1)} %all-gather.6.cloned.1.call-done), kind=kLoop, calls=%fused_computation.4 | loop fusion | flops 16514048 | bytes 11014144 | tf_op jit(solution)/shard_map/reduce_sum | solution.py:23
  121.8 34.6 %all-gather.8.cloned.1.call-done = bf16[5376,256]{1,0:T(8,128)(2,1)} async-done(((bf16[1344,256]{1,0:T(8,128)(2,1)}), bf16[5376,256]{1,0:T(8,128)(2,1)}) %all-gather.8.cloned.1.call-update) | async-done | bytes 2752528 | tf_op jit(solution)/shard_map/all_gather | solution.py:65
  156.4 7.6 %multiply_reduce_fusion.1 = (f32[1024,2]{0,1:T(2,128)S(1)}, f32[1024,256]{0,1:T(8,128)S(1)}) fusion(bf16[5376,256]{1,0:T(8,128)(2,1)} %all-gather.8.cloned.1.call-done, bf16[1024,5376]{1,0:T(8,128)(2,1)} %all-gather.6.cloned.1.call-done, f32[5376]{0:T(1024)S(1)} %copy-done.5, f32[1024]{0:T(1024)S(1)} %add_rsqrt_fusion.2), kind=kOutput, calls=%fused_computation.48 | convolution fusion | flops 2841114624 | bytes 14844928 | tf_op jit(solution)/shard_map/dot_general | solution.py:62
  164.7 34.3 %all-gather.10.cloned.1.call-done = bf16[5376,256]{1,0:T(8,128)(2,1)} async-done(((bf16[1344,256]{1,0:T(8,128)(2,1)}), bf16[5376,256]{1,0:T(8,128)(2,1)}) %all-gather.10.cloned.1.call-update) | async-done | bytes 2752528 | tf_op jit(solution)/shard_map/all_gather | solution.py:66
  199.0 8.0 %fusion.24 = bf16[1,1024,256]{2,1,0:T(8,128)(2,1)S(1)} fusion(bf16[5376,256]{1,0:T(8,128)(2,1)} %all-gather.10.cloned.1.call-done, bf16[1024,5376]{1,0:T(8,128)(2,1)} %all-gather.6.cloned.1.call-done, f32[5376]{0:T(1024)S(1)} %copy-done.5, f32[1024]{0:T(1024)S(1)} %add_rsqrt_fusion.2), kind=kOutput, calls=%fused_computation.40 | convolution fusion | flops 2840854528 | bytes 14312448 | tf_op jit(solution)/shard_map/dot_general | solution.py:62
  207.2 4.4 collective-permute-start
  211.5 67.1 %all-gather.12.cloned.1.call-done = bf16[5376,512]{1,0:T(8,128)(2,1)} async-done(((bf16[1344,512]{1,0:T(8,128)(2,1)}), bf16[5376,512]{1,0:T(8,128)(2,1)}) %all-gather.12.cloned.1.call-update) | async-done | bytes 5505040 | tf_op jit(solution)/shard_map/all_gather | solution.py:64
  278.6 10.8 %multiply_reduce_fusion = (f32[1024,4]{0,1:T(4,128)S(1)}, f32[1024,512]{0,1:T(8,128)S(1)}) fusion(bf16[5376,512]{1,0:T(8,128)(2,1)} %all-gather.12.cloned.1.call-done, bf16[1024,5376]{1,0:T(8,128)(2,1)} %all-gather.6.cloned.1.call-done, f32[5376]{0:T(1024)S(1)} %copy-done.5, f32[1024]{0:T(1024)S(1)} %add_rsqrt_fusion.2), kind=kOutput, calls=%fused_computation.36 | convolution fusion | flops 5660209152 | bytes 18654208 | tf_op jit(solution)/shard_map/dot_general | solution.py:62
  289.4 0.5 multiply_multiply_fusion
  289.9 0.3 multiply_subtract_fusion
  290.5 1.1 fusion.52
  291.6 1.4 maximum_maximum_fusion
  293.2 1.1 slice.66
  295.1 10.4 %fusion.59 = (f32[2,2,512]{2,1,0:T(2,128)S(1)}, f32[2,2,512,1536]{2,3,1,0:T(8,128)}) fusion(bf16[512,2,2,128]{0,3,2,1:T(8,128)(2,1)} %bitcast.69, pred[512,1536]{0,1:T(8,128)(4,1)} %and_and_fusion.1, bf16[1536,2,128,1]{2,1,0,3:T(2,128)(2,1)} %bitcast.67), kind=kOutput, calls=%fused_computation.82 | convolution fusion | flops 814745088 | bytes 14688256 | tf_op jit(solution)/shard_map/sub | solution.py:116
  305.5 10.4 %fusion.54 = (f32[2,2,512]{2,1,0:T(2,128)S(1)}, f32[2,2,512,1536]{2,3,1,0:T(8,128)}) fusion(bf16[512,2,2,128]{0,3,2,1:T(8,128)(2,1)} %bitcast.68, pred[512,1536]{0,1:T(8,128)(4,1)S(1)} %copy-done.1, bf16[1536,2,128,1]{2,1,0,3:T(2,128)(2,1)S(1)} %bitcast.66), kind=kOutput, calls=%fused_computation.81 | convolution fusion | flops 814745088 | bytes 14688256 | tf_op jit(solution)/shard_map/sub | solution.py:116
  315.8 5.7 %fusion.23 = bf16[2,128,2,512]{3,1,2,0:T(8,128)(2,1)S(1)} fusion(bf16[1536,2,128,1]{0,2,3,1:T(8,128)(2,1)S(1)} %bitcast.64, f32[2,2,512,1536]{2,3,1,0:T(8,128)} %get-tuple-element.28, f32[2,2,512]{2,1,0:T(2,128)S(1)} %get-tuple-element.27), kind=kOutput, calls=%fused_computation.38 | convolution fusion | flops 811859968 | bytes 13901824 | tf_op jit(solution)/shard_map/jgqk,kjd->qjgd/dot_general | solution.py:119
  321.5 2.4 copy-done.6
  324.0 1.2 fusion.22
  325.2 18.7 %all-gather.14.cloned.1.call-done = bf16[512,5376]{1,0:T(8,128)(2,1)} async-done(((bf16[128,5376]{1,0:T(8,128)(2,1)}), bf16[512,5376]{1,0:T(8,128)(2,1)}) %all-gather.14.cloned.1.call-update) | async-done | bytes 5505040 | tf_op jit(solution)/shard_map/all_gather | solution.py:124
  344.0 11.2 %convolution_convert_fusion = bf16[1024,5376]{1,0:T(8,128)(2,1)} fusion(bf16[512,5376]{1,0:T(8,128)(2,1)} %all-gather.14.cloned.1.call-done, bf16[512,512]{0,1:T(8,128)(2,1)S(1)} %bitcast.71, bf16[512,512]{0,1:T(8,128)(2,1)S(1)} %bitcast.70), kind=kOutput, calls=%fused_computation.13 | convolution fusion | flops 5644746752 | bytes 17563648 | tf_op jit(solution)/shard_map/dot_general | solution.py:125
  355.2 114.5 %reduce-scatter.2.cloned.1.call-done = bf16[128,5376]{1,0:T(8,128)(2,1)} async-done(((bf16[1024,5376]{1,0:T(8,128)(2,1)}), bf16[128,5376]{1,0:T(8,128)(2,1)}) %reduce-scatter.2.cloned.1.call-update) | async-done | bytes 1376272 | tf_op jit(solution)/shard_map/reduce_scatter | solution.py:128
  469.7 1.7 fusion.17
  471.5 3.0 fusion.20
  (42 shorter events, 2.3 us)
Async XLA Ops:
  6.5 108.9 %all-gather.6.cloned.1.call-start = ((), (), s32[]{:S(2)}) async-start(), calls=%async_computation.1 | async-start | bytes 12386304 | tf_op jit(solution)/shard_map/all_gather | solution.py:57
  7.3 149.1 %all-gather.8.cloned.1.call-start = ((), (), s32[]{:S(2)}) async-start(), calls=%async_computation.2 | async-start | bytes 3440640 | tf_op jit(solution)/shard_map/all_gather | solution.py:65
  8.0 191.0 %all-gather.10.cloned.1.call-start = ((), (), s32[]{:S(2)}) async-start(), calls=%async_computation.3 | async-start | bytes 3440640 | tf_op jit(solution)/shard_map/all_gather | solution.py:66
  8.7 269.9 %all-gather.12.cloned.1.call-start = ((), (), s32[]{:S(2)}) async-start(), calls=%async_computation.4 | async-start | bytes 6881280 | tf_op jit(solution)/shard_map/all_gather | solution.py:64
  9.3 334.7 %all-gather.14.cloned.1.call-start = ((), (), s32[]{:S(2)}) async-start(), calls=%async_computation.5 | async-start | bytes 6881280 | tf_op jit(solution)/shard_map/all_gather | solution.py:124
  9.9 459.8 %reduce-scatter.2.cloned.1.call-start = ((), (), s32[]{:S(2)}) async-start(), calls=%async_computation.6 | async-start | bytes 12386304 | tf_op jit(solution)/shard_map/reduce_scatter | solution.py:128
  14.8 141.6 %copy-start.5 = (f32[5376]{0:T(1024)S(1)}, f32[5376]{0:T(1024)}, u32[]{:S(2)}) copy-start(f32[5376]{0:T(1024)} %param.10) | copy-start | bytes 64516
  121.8 42.3 %copy-start.3 = (f32[128]{0:T(128)S(1)}, f32[128]{0:T(128)}, u32[]{:S(2)}) copy-start(f32[128]{0:T(128)} %param.15) | copy-start | bytes 1540
  207.2 82.3 %copy-start.4 = (f32[128]{0:T(128)S(1)}, f32[128]{0:T(128)}, u32[]{:S(2)}) copy-start(f32[128]{0:T(128)} %param.14) | copy-start | bytes 1540
  207.2 84.4 %collective-permute-start = (bf16[2,1024,256]{2,1,0:T(8,128)(2,1)S(1)}, bf16[2,1024,256]{2,1,0:T(8,128)(2,1)}, u32[]{:S(2)}, u32[]{:S(2)}) collective-permute-start(bf16[2,1024,256]{2,1,0:T(8,128)(2,1)S(1)} %pad_maximum_fusion), channel_id=1, source_target_pairs={{0,8},{8,16},{16,24},{1,9},{9,17},{17,25},{2,10},{10,18},{18,26},{... | collective-permute-start | bytes 3145736 | tf_op jit(solution)/shard_map/ppermute | solution.py:19
  295.1 10.4 %copy-start.1 = (pred[512,1536]{0,1:T(8,128)(4,1)S(1)}, pred[512,1536]{0,1:T(8,128)(4,1)}, u32[]{:S(2)}) copy-start(pred[512,1536]{0,1:T(8,128)(4,1)} %and_and_fusion) | copy-start | bytes 2359300
  315.8 8.2 %copy-start.6 = (f32[2,2,512,1536]{2,3,1,0:T(8,128)S(1)}, f32[2,2,512,1536]{2,3,1,0:T(8,128)}, u32[]{:S(2)}) copy-start(f32[2,2,512,1536]{2,3,1,0:T(8,128)} %get-tuple-element.26) | copy-start | bytes 37748740
  355.2 116.3 %copy-start = (bf16[128,5376]{1,0:T(8,128)(2,1)S(1)}, bf16[128,5376]{1,0:T(8,128)(2,1)}, u32[]{:S(2)}) copy-start(bf16[128,5376]{1,0:T(8,128)(2,1)} %param.9) | copy-start | bytes 4128772
  355.2 116.3 %copy-start.2 = (f32[5376]{0:T(1024)S(1)}, f32[5376]{0:T(1024)}, u32[]{:S(2)}) copy-start(f32[5376]{0:T(1024)} %param.17) | copy-start | bytes 64516
Sparse Core Ops, SparseCore 0:
  9.0 106.4 all-gather.5
  117.3 39.0 all-gather.7
  158.2 40.7 all-gather.9
  200.7 77.8 all-gather.11
  280.3 63.6 all-gather.13
  355.3 114.3 reduce-scatter.1
where the time goes:
time: 482 us; the launch traced here: 481 us
  waiting for transfers between devices  373 us (77%)
  matrix products  65.3 us (14%)
  other arithmetic  18.7 us (4%)
  between operations  13.7 us (3%)
  local copies, waits for them, and re-layouts  5.84 us (1%)
    reduce_scatter x1, waiting for transfers between devices, body(): lax.psum_scatter(lax.optimization_barrier(partial_value).astype(jnp.float...  115 us
    all_gather x1, waiting for transfers between devices, body(): raw_rows = lax.all_gather(hidden_in, 'head', axis=0, tiled=True)  101 us
    all_gather x1, waiting for transfers between devices, body(): query_raw = add_rows(lax.all_gather(w_query, 'ctx', axis=0, tiled=True))  67.1 us
    all_gather x1, waiting for transfers between devices, body(): key_unnormed = add_rows(lax.all_gather(w_key, 'ctx', axis=0, tiled=True))  34.6 us
    all_gather x1, waiting for transfers between devices, body(): lax.all_gather(value_weight, 'ctx', axis=0, tiled=True)  34.3 us
    dot_general x3, matrix products, add_rows(): return jnp.dot(normed, weight_piece, preferred_element_type=jnp.float32)  26.4 us
    sub x2, matrix products, body(): weights = jnp.exp(scores - row_max)  20.7 us
    all_gather x1, waiting for transfers between devices, body(): out_weight = lax.all_gather(w_output, 'ctx', axis=0, tiled=True)  18.7 us
  transfers between devices with their start and end apart: 7, of which 6 were waited for; matrix products, arithmetic and copies ran while one was open for 15% of the time, Pallas kernels for 0%

commit v1 on v0

--- a/solution.py
+++ b/solution.py
@@ -1,6 +1,8 @@
 import jax
 import jax.numpy as jnp
 from jax import lax
+from jax.experimental import pallas as pl
+from jax.experimental.pallas import tpu as pltpu
 from jax.sharding import PartitionSpec as P
 
 HEAD_SIZE = 128
@@ -11,6 +13,414 @@
 query_scale = 168.0 ** (-0.5)
 rope_base = 10000.0
 mask_value = -1e30
+COLUMN_TILE = 768
+PIECES = 2
+
+
+def ring_place(index, count):
+    major, minor = index // 2, index % 2
+    return major + minor * (count - 1 - 2 * major)
+
+
+def ring_index(place, count):
+    second = place // (count // 2)
+    return (1 - second) * (2 * place) + second * (2 * (count - 1 - place) + 1)
+
+
+def gather_kernel(
+    count, chips, hidden, *refs
+):
+    shards, hidden_out, wholes = refs[:3], refs[3], refs[4:7]
+    local_sem, head_send, head_recv, sib_send, sib_recv, ring_send, ring_recv = refs[7:]
+    ctx = lax.axis_index("ctx")
+    head = lax.axis_index("head")
+    chip, core = head // 2, head % 2
+    sibling = chip * 2 + 1 - core
+    upper, lower = head + 2, head - 2
+    has_upper, has_lower = chip < chips - 1, chip > 0
+    place = ring_place(ctx, count)
+    ahead = ring_index((place + 1) % count, count)
+    behind = ring_index((place + count - 1) % count, count)
+    rows = hidden.shape[0]
+
+    barrier = pltpu.get_barrier_semaphore()
+    pl.semaphore_signal(barrier, inc=1, device_id={"head": sibling})
+    pl.semaphore_signal(barrier, inc=1, device_id={"ctx": ahead})
+    pl.semaphore_signal(barrier, inc=1, device_id={"ctx": behind})
+
+    @pl.when(has_upper)
+    def _():
+        pl.semaphore_signal(barrier, inc=1, device_id={"head": upper})
+
+    @pl.when(has_lower)
+    def _():
+        pl.semaphore_signal(barrier, inc=1, device_id={"head": lower})
+
+    pl.semaphore_wait(barrier, 3 + has_upper.astype(jnp.int32) + has_lower.astype(jnp.int32))
+
+    def head_block(owner):
+        return hidden_out.at[pl.ds(pl.multiple_of(owner * rows, rows), rows)]
+
+    def chain_copy(way, distance, target, owner, source=None):
+        block = head_block(owner)
+        return pltpu.make_async_remote_copy(
+            src_ref=block if source is None else source,
+            dst_ref=block,
+            send_sem=head_send.at[way, distance],
+            recv_sem=head_recv.at[way, distance],
+            device_id={"head": target},
+        )
+
+    def sibling_copy(owner, slot, source=None):
+        block = head_block(owner)
+        return pltpu.make_async_remote_copy(
+            src_ref=block if source is None else source,
+            dst_ref=block,
+            send_sem=sib_send.at[slot],
+            recv_sem=sib_recv.at[slot],
+            device_id={"head": sibling},
+        )
+
+    def ring_copy(way, which, distance, half, target, owner, source=None):
+        length = shards[which].shape[0]
+        part = length // 2
+        at = pl.multiple_of(owner * length + half * part, 16)
+        block = wholes[which].at[pl.ds(at, part)]
+        return pltpu.make_async_remote_copy(
+            src_ref=block if source is None else shards[which].at[pl.ds(half * part, part)],
+            dst_ref=block,
+            send_sem=ring_send.at[way, which, distance, half],
+            recv_sem=ring_recv.at[way, which, distance, half],
+            device_id={"ctx": target},
+        )
+
+    @pl.when(has_upper)
+    def _():
+        chain_copy(0, 0, upper, head, hidden).start()
+
+    @pl.when(has_lower)
+    def _():
+        chain_copy(1, 0, lower, head, hidden).start()
+
+    targets = (ahead, behind)
+    for which in range(3):
+        for turn in range(2):
+            for way in range(2):
+                half = turn if way == 0 else 1 - turn
+                ring_copy(way, which, 0, half, targets[way], ctx, True).start()
+    sibling_copy(head, chip, hidden).start()
+    own_copies = [pltpu.make_async_copy(hidden, head_block(head), local_sem.at[3])]
+    for which in range(3):
+        length = shards[which].shape[0]
+        own_copies.append(
+            pltpu.make_async_copy(
+                shards[which],
+                wholes[which].at[pl.ds(pl.multiple_of(ctx * length, 16), length)],
+                local_sem.at[which],
+            )
+        )
+    for copy in own_copies:
+        copy.start()
+
+    def head_step(distance):
+        below = head - 2 * distance
+        above = head + 2 * distance
+
+        @pl.when(chip >= distance)
+        def _():
+            chain_copy(0, distance - 1, upper, below).wait_recv()
+
+            @pl.when(has_upper)
+            def _():
+                if distance < chips - 1:
+                    chain_copy(0, distance, upper, below).start()
+
+            sibling_copy(below, chip - distance).start()
+
+        @pl.when(chip + distance < chips)
+        def _():
+            chain_copy(1, distance - 1, lower, above).wait_recv()
+
+            @pl.when(has_lower)
+            def _():
+                if distance < chips - 1:
+                    chain_copy(1, distance, lower, above).start()
+
+            sibling_copy(above, chip + distance).start()
+
+    def ring_owner(way, distance):
+        step = count - distance if way == 0 else distance
+        return ring_index((place + step) % count, count)
+
+    def ring_halves(distance, way):
+        if distance == count // 2:
+            return (0,) if way == 0 else (1,)
+        return (0, 1) if way == 0 else (1, 0)
+
+    def ring_step(distance):
+        for which in range(3):
+            for turn in range(2):
+                for way in range(2):
+                    halves = ring_halves(distance, way)
+                    if turn >= len(halves):
+                        continue
+                    half = halves[turn]
+                    owner = ring_owner(way, distance)
+                    ring_copy(way, which, distance - 1, half, targets[way], owner).wait_recv()
+                    if distance < count // 2 and half in ring_halves(distance + 1, way):
+                        ring_copy(way, which, distance, half, targets[way], owner).start()
+
+    for distance in range(1, max(chips, count // 2 + 1)):
+        if distance < chips:
+            head_step(distance)
+        if distance <= count // 2:
+            ring_step(distance)
+
+    for other in range(chips):
+        sibling_copy(other * 2 + 1 - core, other).wait_recv()
+    for copy in own_copies:
+        copy.wait()
+    for other in range(chips):
+        sibling_copy(other * 2 + core, other).wait_send()
+    for distance in range(chips - 1):
+        @pl.when(has_upper & (chip >= distance))
+        def _():
+            chain_copy(0, distance, upper, head - 2 * distance).wait_send()
+
+        @pl.when(has_lower & (chip + distance < chips))
+        def _():
+            chain_copy(1, distance, lower, head + 2 * distance).wait_send()
+
+    for distance in range(count // 2):
+        for which in range(3):
+            for way in range(2):
+                for half in ring_halves(distance + 1, way):
+                    ring_copy(
+                        way, which, distance, half, targets[way], ring_owner(way, distance)
+                    ).wait_send()
+
+
+def gather_all(hidden_in, w_query, w_key, value_weight):
+    count = lax.axis_size("ctx")
+    chips = lax.axis_size("head") // 2
+    any_spec = pl.BlockSpec(memory_space=pl.ANY)
+
+    def grown(shard, times):
+        return jax.ShapeDtypeStruct((shard.shape[0] * times, shard.shape[1]), shard.dtype)
+
+    dma = pltpu.SemaphoreType.DMA
+    return pl.pallas_call(
+        lambda *refs: gather_kernel(count, chips, *refs),
+        out_shape=(
+            grown(hidden_in, 2 * chips),
+            grown(w_query, count),
+            grown(w_key, count),
+            grown(value_weight, count),
+        ),
+        in_specs=[any_spec] * 4,
+        out_specs=(any_spec,) * 4,
+        scratch_shapes=[
+            dma((4,)),
+            dma((2, chips)),
+            dma((2, chips)),
+            dma((chips,)),
+            dma((chips,)),
+            dma((2, 3, count // 2, 2)),
+            dma((2, 3, count // 2, 2)),
+        ],
+        compiler_params=pltpu.CompilerParams(
+            collective_id=0, has_side_effects=True, vmem_limit_bytes=4 * 2**20
+        ),
+    )(hidden_in, w_query, w_key, value_weight)
+
+
+def scatter_kernel(
+    chips,
+    attended,
+    weight,
+    out,
+    part,
+    pair_in,
+    down_in,
+    up_in,
+    pair_send,
+    pair_recv,
+    chain_send,
+    chain_recv,
+):
+    head = lax.axis_index("head")
+    chip, core = head // 2, head % 2
+    sibling = chip * 2 + 1 - core
+    upper, lower = head + 2, head - 2
+    has_upper, has_lower = chip < chips - 1, chip > 0
+    rows = out.shape[0]
+    width = out.shape[1]
+    piece = rows // PIECES
+    tiles = width // COLUMN_TILE
+    mine = pl.multiple_of(core * rows, rows)
+
+    barrier = pltpu.get_barrier_semaphore()
+    pl.semaphore_signal(barrier, inc=1, device_id={"head": sibling})
+
+    @pl.when(has_upper)
+    def _():
+        pl.semaphore_signal(barrier, inc=1, device_id={"head": upper})
+
+    @pl.when(has_lower)
+    def _():
+        pl.semaphore_signal(barrier, inc=1, device_id={"head": lower})
+
+    pl.semaphore_wait(barrier, 1 + has_upper.astype(jnp.int32) + has_lower.astype(jnp.int32))
+
+    def pair_copy(target):
+        return pltpu.make_async_remote_copy(
+            src_ref=part.at[target, pl.ds(pl.multiple_of((1 - core) * rows, rows), rows)],
+            dst_ref=pair_in.at[target],
+            send_sem=pair_send.at[target],
+            recv_sem=pair_recv.at[target],
+            device_id={"head": sibling},
+        )
+
+    landing = (up_in, down_in)
+
+    def chain_copy(way, target, at):
+        return pltpu.make_async_remote_copy(
+            src_ref=part.at[target, pl.ds(pl.multiple_of(mine + at * piece, piece), piece)],
+            dst_ref=landing[way].at[target, pl.ds(at * piece, piece)],
+            send_sem=chain_send.at[way, target, at],
+            recv_sem=chain_recv.at[way, target, at],
+            device_id={"head": upper if way == 0 else lower},
+        )
+
+    def project(target):
+        start = pl.multiple_of(target * 2 * rows, 2 * rows)
+
+        @pl.loop(0, tiles)
+        def _(tile):
+            columns = pl.ds(pl.multiple_of(tile * COLUMN_TILE, COLUMN_TILE), COLUMN_TILE)
+            part[target, :, columns] = jnp.dot(
+                attended[pl.ds(start, 2 * rows), :],
+                weight[:, columns],
+                preferred_element_type=jnp.float32,
+            ).astype(jnp.bfloat16)
+
+        pair_copy(target).start()
+
+    def targets_at(step):
+        return step + chip - (chips - 1), chips - 1 - step + chip
+
+    def compute(step):
+        if step == chips - 1:
+            project(chip)
+        elif step < chips - 1:
+            down, up = targets_at(step)
+
+            @pl.when(down >= 0)
+            def _():
+                project(down)
+
+            @pl.when(up < chips)
+            def _():
+                project(up)
+
+    def add_into(way, target, at, with_chain):
+        spot = pl.ds(pl.multiple_of(mine + at * piece, piece), piece)
+        near = pl.ds(at * piece, piece)
+
+        @pl.loop(0, tiles)
+        def _(tile):
+            columns = pl.ds(pl.multiple_of(tile * COLUMN_TILE, COLUMN_TILE), COLUMN_TILE)
+            value = part[target, spot, columns].astype(jnp.float32)
+            value += pair_in[target, near, columns].astype(jnp.float32)
+            if with_chain:
+                value += landing[way][target, near, columns].astype(jnp.float32)
+            part[target, spot, columns] = value.astype(jnp.bfloat16)
+
+    def relay(way, target):
+        source_there = has_lower if way == 0 else has_upper
+        pair_copy(target).wait_recv()
+        for at in range(PIECES):
+            @pl.when(source_there)
+            def _():
+                chain_copy(way, target, at).wait_recv()
+                add_into(way, target, at, True)
+
+            @pl.when(jnp.logical_not(source_there))
+            def _():
+                add_into(way, target, at, False)
+
+            chain_copy(way, target, at).start()
+
+    compute(0)
+    compute(1)
+    for step in range(chips - 1):
+        down, up = targets_at(step)
+
+        @pl.when(down >= 0)
+        def _():
+            relay(1, down)
+
+        @pl.when(up < chips)
+        def _():
+            relay(0, up)
+
+        compute(step + 2)
+
+    pair_copy(chip).wait_recv()
+
+    @pl.loop(0, tiles)
+    def _(tile):
+        columns = pl.ds(pl.multiple_of(tile * COLUMN_TILE, COLUMN_TILE), COLUMN_TILE)
+        out[:, columns] = part[chip, pl.ds(mine, rows), columns].astype(jnp.float32) + pair_in[
+            chip, :, columns
+        ].astype(jnp.float32)
+
+    for way, there in ((0, has_lower), (1, has_upper)):
+        @pl.when(there)
+        def _():
+            for at in range(PIECES):
+                chain_copy(way, chip, at).wait_recv()
+
+            @pl.loop(0, tiles)
+            def _(tile):
+                columns = pl.ds(pl.multiple_of(tile * COLUMN_TILE, COLUMN_TILE), COLUMN_TILE)
+                out[:, columns] += landing[way][chip, :, columns].astype(jnp.float32)
+
+    for target in range(chips):
+        pair_copy(target).wait_send()
+
+    for step in range(chips - 1):
+        for way, target in ((1, step + chip - (chips - 1)), (0, chips - 1 - step + chip)):
+            @pl.when((target >= 0) & (target < chips))
+            def _():
+                for at in range(PIECES):
+                    chain_copy(way, target, at).wait_send()
+
+
+def project_and_scatter(attended, out_weight):
+    chips = lax.axis_size("head") // 2
+    rows = attended.shape[0] // (2 * chips)
+    width = out_weight.shape[1]
+    dma = pltpu.SemaphoreType.DMA
+    return pl.pallas_call(
+        lambda *refs: scatter_kernel(chips, *refs),
+        out_shape=jax.ShapeDtypeStruct((rows, width), jnp.float32),
+        in_specs=[pl.BlockSpec(memory_space=pltpu.VMEM)] * 2,
+        out_specs=pl.BlockSpec(memory_space=pltpu.VMEM),
+        scratch_shapes=[
+            pltpu.VMEM((chips, 2 * rows, width), jnp.bfloat16),
+            pltpu.VMEM((chips, rows, width), jnp.bfloat16),
+            pltpu.VMEM((chips, rows, width), jnp.bfloat16),
+            pltpu.VMEM((chips, rows, width), jnp.bfloat16),
+            dma((chips,)),
+            dma((chips,)),
+            dma((2, chips, PIECES)),
+            dma((2, chips, PIECES)),
+        ],
+        compiler_params=pltpu.CompilerParams(
+            collective_id=1, has_side_effects=True, vmem_limit_bytes=54 * 2**20
+        ),
+    )(attended, out_weight)
 
 
 def passed_along(shard, axis, by):
@@ -54,16 +464,20 @@
     post_gain,
 ):
     own_rows = hidden_in.astype(jnp.float32)
-    raw_rows = lax.all_gather(hidden_in, "head", axis=0, tiled=True)
+    raw_rows, whole_query, whole_key, whole_value = gather_all(
+        hidden_in, w_query, w_key, value_weight
+    )
+    w_output, raw_rows = lax.optimization_barrier((w_output, raw_rows))
+    out_weight = lax.all_gather(w_output, "ctx", axis=0, tiled=True)
     normed = root_mean_scale(raw_rows.astype(jnp.float32), pre_gain).astype(jnp.bfloat16)
     tok_count = normed.shape[0]
 
-    def add_rows(weight_piece):
-        return jnp.dot(normed, weight_piece, preferred_element_type=jnp.float32)
-
-    query_raw = add_rows(lax.all_gather(w_query, "ctx", axis=0, tiled=True))
-    key_unnormed = add_rows(lax.all_gather(w_key, "ctx", axis=0, tiled=True))
-    value_unnormed = add_rows(lax.all_gather(value_weight, "ctx", axis=0, tiled=True))
+    def add_rows(weight):
+        return jnp.dot(normed, weight, preferred_element_type=jnp.float32)
+
+    query_raw = add_rows(whole_query)
+    key_unnormed = add_rows(whole_key)
+    value_unnormed = add_rows(whole_value)
     local_heads = w_query.shape[1] // HEAD_SIZE
     local_groups = w_key.shape[1] // HEAD_SIZE
     heads_per_group = local_heads // local_groups
@@ -121,16 +535,7 @@
         )
         outputs.append(mixed.astype(jnp.bfloat16).reshape(block_rows, local_heads * HEAD_SIZE))
     attended = jnp.concatenate(outputs, axis=0)
-    out_weight = lax.all_gather(w_output, "ctx", axis=0, tiled=True)
-    partial_value = jnp.dot(attended, out_weight, preferred_element_type=jnp.float32).astype(
-        jnp.bfloat16
-    )
-    summed = lax.psum_scatter(
-        lax.optimization_barrier(partial_value).astype(jnp.float32).astype(jnp.bfloat16),
-        "head",
-        scatter_dimension=0,
-        tiled=True,
-    ).astype(jnp.float32)
+    summed = project_and_scatter(attended, out_weight)
     result = own_rows + root_mean_scale(summed, post_gain)
     return result.astype(jnp.bfloat16)
 

time: 482 us -> 330 us (0.68)
  waiting for transfers between devices: 373 us -> 20.5 us
  Pallas kernels: 0 us -> 200 us
  matrix products: 65.3 us -> 55.9 us
  local copies, waits for them, and re-layouts: 5.84 us -> 15.2 us
    all_gather x4 -> x0, waiting for transfers between devices: 237 us -> none  [the longest x1 101 us: body(): raw_rows = lax.all_gather(hidden_in, 'head', axis=0, tiled=True)]
    pallas_call x0 -> x2, Pallas kernels: none -> 200 us  [the longest x1 101 us: project_and_scatter(): pl.pallas_call(lambda *refs: scatter_kernel(chips, *refs), out_shape=jax....]
    reduce_scatter x1 -> x0, waiting for transfers between devices: 115 us -> none  [body(): lax.psum_scatter(lax.optimization_barrier(partial_value).astype(jnp.float...]
    ppermute x1, waiting for transfers between devices: 0.01 us -> 20 us  [passed_along(): return lax.ppermute(shard, axis, pairs)]
    all_gather x1, waiting for transfers between devices: 18.7 us -> 0.42 us  [body(): out_weight = lax.all_gather(w_output, 'ctx', axis=0, tiled=True)]
    dot_general x4 -> x3, matrix products: 37.6 us -> 24.5 us  [add_rows(): return jnp.dot(normed, weight, preferred_element_type=jnp.float32)]
    unnamed x14 -> x34, local copies, waits for them, and re-layouts: 2.46 us -> 10.5 us
  transfers between devices with their start and end apart: 7 -> 2, of which waited for: 6 -> 2; matrix products, arithmetic and copies ran while one was open for 15% -> 16% of each run, Pallas kernels for 0% -> 0%
where the time goes in v1:
time: 330 us; the launch traced here: 328 us
  Pallas kernels  200 us (61%)
  matrix products  55.9 us (17%)
  waiting for transfers between devices  20.5 us (6%)
  other arithmetic  18.6 us (6%)
  local copies, waits for them, and re-layouts  15.2 us (5%)
  between operations  13.7 us (4%)
  starting transfers between devices  4.43 us (1%)
    pallas_call x1, Pallas kernels, project_and_scatter(): pl.pallas_call(lambda *refs: scatter_kernel(chips, *refs), out_shape=jax....  101 us
    pallas_call x1, Pallas kernels, gather_all(): pl.pallas_call(lambda *refs: gather_kernel(count, chips, *refs), out_shap...  99 us
    dot_general x3, matrix products, add_rows(): return jnp.dot(normed, weight, preferred_element_type=jnp.float32)  24.5 us
    ppermute x1, waiting for transfers between devices, passed_along(): return lax.ppermute(shard, axis, pairs)  20 us
    sub x2, matrix products, body(): weights = jnp.exp(scores - row_max)  19.9 us
    dot_general x2, matrix products, body(): jnp.einsum('jgqk,kjd->qjgd', probabilities, value_block, preferred_elemen...  11.5 us
    unnamed x34, local copies, waits for them, and re-layouts  10.5 us
  transfers between devices with their start and end apart: 2, of which 2 were waited for; matrix products, arithmetic and copies ran while one was open for 16% of the time, Pallas kernels for 0%

profile of v1, /device:TPU:0, one launch (start us, length us, event | category | flops | bytes accessed | tf_op | source)
XLA Modules:
  0.0 328.3 jit_solution(2041234985424816052)
XLA Ops:
  6.6 1.3 copy-done.1
  7.9 1.3 copy-done.3
  9.2 1.1 copy-done.4
  10.3 1.1 copy-done.5
  11.4 99.0 %shard_map.91 = (bf16[1024,5376]{1,0:T(8,128)(2,1)S(1)}, bf16[5376,512]{1,0:T(8,128)(2,1)S(1)}, bf16[5376,256]{1,0:T(8,128)(2,1)S(1)}, bf16[5376,256]{1,0:T(8,128)(2,1)S(1)}) custom-call(bf16[128,5376]{1,0:T(8,128)(2,1)S(1)} %copy-done.1, bf16[1344,512]{1,0:T(8,128)(2,1)S(1)} %copy-done.3, bf16[1344,256]{1,0:T(8,128)(2,1)S(1)} %copy-done.4, ...), custom_call_target="tpu_custom_call" | custom-call | tf_op jit(solution)/shard_map/pallas_call | solution.py:212
  110.5 2.5 copy-done.6
  112.9 1.5 copy-done.7
  114.5 1.6 copy-done.8
  116.1 2.2 fusion.2
  118.3 7.3 %fusion.20 = bf16[1,1024,256]{2,1,0:T(8,128)(2,1)} fusion(bf16[5376,256]{1,0:T(8,128)(2,1)} %copy-done.8, bf16[1024,5376]{1,0:T(8,128)(2,1)S(1)} %get-tuple-element.12, f32[5376]{0:T(1024)S(1)} %copy-done.16, f32[1024]{0:T(1024)S(1)} %add_rsqrt_fusion.2), kind=kOutput, calls=%fused_computation.35 | convolution fusion | flops 2840854528 | bytes 14312448 | tf_op jit(solution)/shard_map/dot_general | solution.py:476
  125.6 6.3 %multiply_reduce_fusion.2 = (f32[1024,2]{0,1:T(2,128)S(1)}, f32[1024,256]{0,1:T(8,128)}) fusion(bf16[5376,256]{1,0:T(8,128)(2,1)} %copy-done.7, bf16[1024,5376]{1,0:T(8,128)(2,1)S(1)} %get-tuple-element.12, f32[5376]{0:T(1024)S(1)} %copy-done.16, f32[1024]{0:T(1024)S(1)} %add_rsqrt_fusion.2), kind=kOutput, calls=%fused_computation.41 | convolution fusion | flops 2841114624 | bytes 14844928 | tf_op jit(solution)/shard_map/dot_general | solution.py:476
  132.0 1.0 multiply_cosine_fusion
  133.0 1.4 multiply_multiply_fusion.1
  134.8 1.1 pad_maximum_fusion
  135.9 4.4 %collective-permute-start = (bf16[2,1024,256]{2,1,0:T(8,128)(2,1)}, bf16[2,1024,256]{2,1,0:T(8,128)(2,1)}, u32[]{:S(2)}, u32[]{:S(2)}) collective-permute-start(bf16[2,1024,256]{2,1,0:T(8,128)(2,1)} %pad_maximum_fusion), channel_id=1, source_target_pairs={{0,8},{8,16},{16,24},{1,9},{9,17},{17,25},{2,10},{10,18},{18,26},{... | collective-permute-start | bytes 3145736 | tf_op jit(solution)/shard_map/ppermute | solution.py:429
  140.3 10.8 %multiply_reduce_fusion.1 = (f32[1024,4]{0,1:T(4,128)S(1)}, f32[1024,512]{0,1:T(8,128)S(1)}) fusion(bf16[5376,512]{1,0:T(8,128)(2,1)} %copy-done.6, bf16[1024,5376]{1,0:T(8,128)(2,1)} %copy-done, f32[5376]{0:T(1024)S(1)} %copy-done.16, f32[1024]{0:T(1024)S(1)} %add_rsqrt_fusion.2), kind=kOutput, calls=%fused_computation.31 | convolution fusion | flops 5660209152 | bytes 18654208 | tf_op jit(solution)/shard_map/dot_general | solution.py:476
  151.2 0.4 multiply_multiply_fusion
  152.4 1.1 fusion.44
  153.5 1.9 and_and_fusion
  155.4 1.9 and_and_fusion.1
  157.3 20.0 %collective-permute-done = bf16[2,1024,256]{2,1,0:T(8,128)(2,1)} collective-permute-done((bf16[2,1024,256]{2,1,0:T(8,128)(2,1)}, bf16[2,1024,256]{2,1,0:T(8,128)(2,1)}, u32[]{:S(2)}, u32[]{:S(2)}) %collective-permute-start) | collective-permute-done | bytes 1048608 | tf_op jit(solution)/shard_map/ppermute | solution.py:429
  177.3 1.4 maximum_maximum_fusion
  178.9 1.2 copy.32
  180.3 10.0 %fusion.46 = (f32[2,2,512]{2,1,0:T(2,128)S(1)}, f32[2,2,512,1536]{2,3,1,0:T(8,128)}) fusion(bf16[512,2,2,128]{0,3,2,1:T(8,128)(2,1)} %bitcast.70, pred[512,1536]{0,1:T(8,128)(4,1)} %and_and_fusion, bf16[1536,2,128,1]{2,1,0,3:T(2,128)(2,1)S(1)} %bitcast.66), kind=kOutput, calls=%fused_computation.73 | convolution fusion | flops 814745088 | bytes 14688256 | tf_op jit(solution)/shard_map/sub | solution.py:530
  190.3 5.9 %fusion.18 = bf16[2,128,2,512]{3,1,2,0:T(8,128)(2,1)S(1)} fusion(bf16[1536,2,128,1]{0,2,3,1:T(8,128)(2,1)} %bitcast.64, f32[2,2,512,1536]{2,3,1,0:T(8,128)} %get-tuple-element.38, f32[2,2,512]{2,1,0:T(2,128)S(1)} %get-tuple-element.37), kind=kOutput, calls=%fused_computation.32 | convolution fusion | flops 811859968 | bytes 13901824 | tf_op jit(solution)/shard_map/jgqk,kjd->qjgd/dot_general | solution.py:533
  196.4 1.2 copy.28
  197.8 9.9 %fusion.51 = (f32[2,2,512]{2,1,0:T(2,128)S(1)}, f32[2,2,512,1536]{2,3,1,0:T(8,128)}) fusion(bf16[512,2,2,128]{0,3,2,1:T(8,128)(2,1)} %bitcast.69, pred[512,1536]{0,1:T(8,128)(4,1)S(1)} %copy-done.11, bf16[1536,2,128,1]{2,1,0,3:T(2,128)(2,1)S(1)} %bitcast.65), kind=kOutput, calls=%fused_computation.74 | convolution fusion | flops 814745088 | bytes 14688256 | tf_op jit(solution)/shard_map/sub | solution.py:530
  207.7 5.6 %fusion.19 = bf16[2,128,2,512]{3,1,2,0:T(8,128)(2,1)S(1)} fusion(bf16[1536,2,128,1]{0,2,3,1:T(8,128)(2,1)S(1)} %bitcast.63, f32[2,2,512,1536]{2,3,1,0:T(8,128)} %get-tuple-element.40, f32[2,2,512]{2,1,0:T(2,128)S(1)} %get-tuple-element.39), kind=kOutput, calls=%fused_computation.33 | convolution fusion | flops 811859968 | bytes 13901824 | tf_op jit(solution)/shard_map/jgqk,kjd->qjgd/dot_general | solution.py:533
  213.5 1.0 pad_maximum_fusion.1.refs_0_
  215.0 101.1 %shard_map.92 = f32[128,5376]{1,0:T(8,128)} custom-call(bf16[1024,512]{1,0:T(8,128)(2,1)} %pad_maximum_fusion.1.refs_0_, bf16[512,5376]{1,0:T(8,128)(2,1)} %all-gather.2.cloned.1.call-done.refs_1_), custom_call_target="tpu_custom_call" | custom-call | tf_op jit(solution)/shard_map/pallas_call | solution.py:405
  316.1 2.1 multiply_reduce_fusion
  318.1 3.3 %add_convert_fusion = bf16[128,5376]{1,0:T(8,128)(2,1)} fusion(f32[128,5376]{1,0:T(8,128)} %shard_map.92, bf16[128,5376]{1,0:T(8,128)(2,1)S(1)} %copy-done.2, f32[5376]{0:T(1024)S(1)} %copy-done.13, f32[128]{0:T(128)S(1)} %add_rsqrt_fusion.3), kind=kLoop, calls=%fused_computation.25 | loop fusion | flops 3440640 | bytes 5527040 | tf_op jit(solution)/shard_map/convert_element_type | solution.py:540
  (51 shorter events, 2.8 us)
Async XLA Ops:
  6.5 208.4 %all-gather.2.cloned.1.call-start = ((), (), s32[]{:S(2)}) async-start(), calls=%async_computation | async-start | bytes 6881280 | tf_op jit(solution)/shard_map/all_gather | solution.py:471
  6.6 1.3 copy-start.1
  7.9 1.3 copy-start.3
  9.2 1.1 copy-start.4
  10.3 1.1 copy-start.5
  110.5 2.5 copy-start.6
  112.9 1.5 copy-start.7
  114.5 1.6 copy-start.8
  116.1 9.6 %copy-start = (bf16[1024,5376]{1,0:T(8,128)(2,1)}, bf16[1024,5376]{1,0:T(8,128)(2,1)S(1)}, u32[]{:S(2)}) copy-start(bf16[1024,5376]{1,0:T(8,128)(2,1)S(1)} %get-tuple-element.12) | copy-start | bytes 33030148
  116.1 2.2 copy-start.16
  125.6 7.4 %copy-start.14 = (f32[128]{0:T(128)S(1)}, f32[128]{0:T(128)}, u32[]{:S(2)}) copy-start(f32[128]{0:T(128)} %param.15) | copy-start | bytes 1540
  132.0 2.8 copy-start.9
  135.9 41.4 %collective-permute-start = (bf16[2,1024,256]{2,1,0:T(8,128)(2,1)}, bf16[2,1024,256]{2,1,0:T(8,128)(2,1)}, u32[]{:S(2)}, u32[]{:S(2)}) collective-permute-start(bf16[2,1024,256]{2,1,0:T(8,128)(2,1)} %pad_maximum_fusion), channel_id=1, source_target_pairs={{0,8},{8,16},{16,24},{1,9},{9,17},{17,25},{2,10},{10,18},{18,26},{... | collective-permute-start | bytes 3145736 | tf_op jit(solution)/shard_map/ppermute | solution.py:429
  140.3 10.9 %copy-start.15 = (f32[128]{0:T(128)S(1)}, f32[128]{0:T(128)}, u32[]{:S(2)}) copy-start(f32[128]{0:T(128)} %param.14) | copy-start | bytes 1540
  151.6 25.6 %copy-start.10 = (bf16[1,1024,256]{2,1,0:T(8,128)(2,1)S(1)}, bf16[1,1024,256]{2,1,0:T(8,128)(2,1)}, u32[]{:S(2)}) copy-start(bf16[1,1024,256]{2,1,0:T(8,128)(2,1)} %fusion.20) | copy-start | bytes 1572868
  190.3 7.5 %copy-start.11 = (pred[512,1536]{0,1:T(8,128)(4,1)S(1)}, pred[512,1536]{0,1:T(8,128)(4,1)}, u32[]{:S(2)}) copy-start(pred[512,1536]{0,1:T(8,128)(4,1)} %and_and_fusion.1) | copy-start | bytes 2359300
  197.8 9.9 %copy-start.12 = (bf16[1,1536,256]{1,2,0:T(8,128)(2,1)S(1)}, bf16[1,1536,256]{1,2,0:T(8,128)(2,1)}, u32[]{:S(2)}) copy-start(bf16[1,1536,256]{1,2,0:T(8,128)(2,1)} %copy.28) | copy-start | bytes 2359300
  214.5 103.6 %copy-start.2 = (bf16[128,5376]{1,0:T(8,128)(2,1)S(1)}, bf16[128,5376]{1,0:T(8,128)(2,1)}, u32[]{:S(2)}) copy-start(bf16[128,5376]{1,0:T(8,128)(2,1)} %refs_0_.1) | copy-start | bytes 4128772
  214.5 103.6 %copy-start.13 = (f32[5376]{0:T(1024)S(1)}, f32[5376]{0:T(1024)}, u32[]{:S(2)}) copy-start(f32[5376]{0:T(1024)} %param.17) | copy-start | bytes 64516
Sparse Core Ops, SparseCore 0:
  140.4 74.4 all-gather.1
